TPU v7x, 256 devices: a whole 4x4x8 slice. The times are simulated.
256 devices in a mesh: dp: 16 (over z, core), fsdp: 16 (over y, x).
Axes of the slice: x: 4, y: 4, z: 8, core: 2. Of those that a mesh axis runs over, the one named last changes fastest.
Arguments:
- tokens: bfloat16 [65536, 8192], P(('dp', 'fsdp')), may hold values from -6 to 6
- cotangent: bfloat16 [65536, 1024], P(('dp', 'fsdp')), may hold values from -6 to 6
- value_weight: bfloat16 [8192, 1024], P('fsdp'), may hold values from -0.1875 to 0.1875
- adapter_down_weight: bfloat16 [64, 8192, 64], P('dp', 'fsdp'), may hold values from -0.0625 to 0.0625
- adapter_up_weight: bfloat16 [64, 64, 1024], P('dp', None, 'fsdp'), may hold values from -0.1875 to 0.1875
- segment_tenant: int32 [16, 8], replicated, may hold values from 0 to 63, as said below
- segment_lengths: int32 [16, 8], replicated, may hold values from 1 to 2048, 4096 in all within a row
- tenant_stored_row: int32 [64], replicated, may hold values from 0 to 63, as said below
Outputs:
- input_gradient: bfloat16 [65536, 8192], P(('dp', 'fsdp'))
- adapter_down_gradient: float32 [64, 8192, 64], P('dp', 'fsdp')
- adapter_up_gradient: float32 [64, 64, 1024], P('dp', None, 'fsdp')
Inputs may be any that keep to these rules, and one draw needn't show every extreme that they name: `segment_tenant`: the 8 tenants of one bin are distinct, and the packer places them so that their stored rows tenant_stored_row[t] lie in 8 different blocks of 4 consecutive rows (no bin draws two tenants whose adapters one dp index owns). A permutation of the tenants: tenant t's adapters are row tenant_stored_row[t] of adapter_down_weight and adapter_up_weight.
All inputs are finite; a program needn't handle non-finite values.
Results may differ from a plain program's by a relative error of at most 0.018.
Values may be sent and summed in bfloat16 or wider, within the bound.
No kernel may reach another device: no remote copies, remote signals or barrier semaphores. Data moves between devices by JAX's collectives and lax.ppermute only.
A program may use at most 128 MiB of HBM per device.

v0:
```python
import jax
import jax.numpy as jnp
from jax import lax
from jax.sharding import PartitionSpec as P

ADAPTER_SCALE = 2.0


def slot_columns(lengths_row, positions, rank_space_width):
    seg_ends = jnp.cumsum(lengths_row)
    starts = seg_ends - lengths_row
    inside = (positions[:, None] >= starts[None, :]) & (positions[:, None] < seg_ends[None, :])
    return jnp.repeat(inside, rank_space_width, axis=1)


def local(
    tokens,
    cotangent,
    value_weight,
    adapter_down_weight,
    adapter_up_weight,
    segment_tenant,
    segment_lengths,
    tenant_stored_row,
):
    local_token_count, model_width_piece, rank_space_width = adapter_down_weight.shape
    value_width_piece = adapter_up_weight.shape[2]
    bin_count, slot_count = segment_tenant.shape
    rows_here = tokens.shape[0]
    groups = lax.axis_size("fsdp")
    me_bin = lax.axis_index("dp")
    me_piece = lax.axis_index("fsdp")
    gradient_norm_value = (groups * rows_here) ** (-0.5)
    zero_constant = jnp.zeros((), jnp.bfloat16)
    contract_last = (((1,), (1,)), ((), ()))
    contract_first = (((0,), (0,)), ((), ()))
    matches = (
        segment_tenant[:, :, None]
        == jnp.arange(tenant_stored_row.shape[0], dtype=jnp.int32)[None, None, :]
    )
    stored = jnp.sum(jnp.where(matches, tenant_stored_row[None, None, :], 0), axis=2)
    my_stored = lax.dynamic_index_in_dim(stored, me_bin, 0, keepdims=False)
    table_down, table_up = (
        lax.all_gather(adapter_down_weight, "dp", axis=0, tiled=True),
        lax.all_gather(adapter_up_weight, "dp", axis=0, tiled=True),
    )
    segment_down_weight = jnp.take(table_down, my_stored, axis=0)
    segment_up_weight = jnp.take(table_up, my_stored, axis=0)
    down_cols = jnp.transpose(segment_down_weight, (1, 0, 2)).reshape(
        model_width_piece, slot_count * rank_space_width
    )
    up_rows = segment_up_weight.reshape(slot_count * rank_space_width, value_width_piece)
    down_full, up_full = (
        lax.all_gather(down_cols, "fsdp", axis=0, tiled=True),
        lax.all_gather(up_rows, "fsdp", axis=1, tiled=True),
    )
    my_lengths = lax.dynamic_index_in_dim(segment_lengths, me_bin, 0, keepdims=False)
    positions = me_piece * rows_here + jnp.arange(rows_here, dtype=jnp.int32)
    broadcast_row_mask = slot_columns(my_lengths, positions, rank_space_width)
    low_rank = jnp.where(
        broadcast_row_mask,
        jnp.dot(tokens, down_full, preferred_element_type=jnp.float32).astype(jnp.bfloat16),
        zero_constant,
    )
    matrix_product = lax.dot_general(
        cotangent, up_full, contract_last, preferred_element_type=jnp.float32
    )
    rank_space_gradient = jnp.where(
        broadcast_row_mask, (ADAPTER_SCALE * matrix_product).astype(jnp.bfloat16), zero_constant
    )
    base_term = lax.dot_general(
        cotangent,
        lax.all_gather(value_weight, "fsdp", axis=0, tiled=True),
        contract_last,
        preferred_element_type=jnp.float32,
    )
    adapter_term = lax.dot_general(
        rank_space_gradient, down_full, contract_last, preferred_element_type=jnp.float32
    )
    input_gradient = (base_term + adapter_term).astype(jnp.bfloat16)
    part_down = lax.dot_general(
        tokens, rank_space_gradient, contract_first, preferred_element_type=jnp.float32
    )
    partial_up_gradient = ADAPTER_SCALE * lax.dot_general(
        low_rank, cotangent, contract_first, preferred_element_type=jnp.float32
    )
    sum_down, sum_up = (
        lax.psum_scatter(
            part_down.astype(jnp.bfloat16), "fsdp", scatter_dimension=0, tiled=True
        ).astype(jnp.float32),
        lax.psum_scatter(
            partial_up_gradient.astype(jnp.bfloat16), "fsdp", scatter_dimension=1, tiled=True
        ).astype(jnp.float32),
    )
    bin_down = jnp.transpose(
        sum_down.astype(jnp.bfloat16).reshape(model_width_piece, slot_count, rank_space_width),
        (1, 0, 2),
    )
    bin_up = sum_up.astype(jnp.bfloat16).reshape(slot_count, rank_space_width, value_width_piece)
    segment_placement = (
        my_stored[:, None] == jnp.arange(bin_count * local_token_count, dtype=jnp.int32)[None, :]
    ).astype(jnp.bfloat16)
    table_down = jnp.einsum(
        "st,sdr->tdr", segment_placement, bin_down, preferred_element_type=jnp.float32
    )
    table_up = jnp.einsum(
        "st,srv->trv", segment_placement, bin_up, preferred_element_type=jnp.float32
    )
    down_grad, up_grad = (
        lax.psum_scatter(
            table_down.astype(jnp.bfloat16), "dp", scatter_dimension=0, tiled=True
        ).astype(jnp.float32),
        lax.psum_scatter(
            table_up.astype(jnp.bfloat16), "dp", scatter_dimension=0, tiled=True
        ).astype(jnp.float32),
    )
    return (input_gradient, down_grad * gradient_norm_value, up_grad * gradient_norm_value)


def solution(mesh):
    placed = (
        P(("dp", "fsdp"), None),
        P(("dp", "fsdp"), None),
        P("fsdp", None),
        P("dp", "fsdp", None),
        P("dp", None, "fsdp"),
        P(),
        P(),
        P(),
    )
    return jax.shard_map(
        local,
        mesh=mesh,
        in_specs=placed,
        out_specs=(P(("dp", "fsdp"), None), P("dp", "fsdp", None), P("dp", None, "fsdp")),
        check_vma=False,
    )
```

profile of v0, /device:TPU:1, one launch (start us, length us, event | category | flops | bytes accessed | tf_op | source)
XLA Modules:
  0.0 626.8 jit_solution(17753394289822480714)
XLA Ops:
  7.2 0.7 all-gather.9.cloned.1.call-update
  8.0 0.8 copy.25
  8.7 1.1 select_reduce_fusion
  9.9 46.4 %all-gather.9.cloned.1.call-done = bf16[64,512,64]{1,2,0:T(8,128)(2,1)} async-done(((bf16[4,512,64]{1,2,0:T(8,128)(2,1)}), bf16[64,512,64]{1,2,0:T(8,128)(2,1)}) %all-gather.9.cloned.1.call-update) | async-done | bytes 4194320 | tf_op jit(solution)/shard_map/all_gather | solution.py:44
  56.2 2.8 gather_fusion.1
  59.0 0.9 broadcast_select_fusion
  60.1 19.3 %all_gather.16 = bf16[64,64,64]{2,1,0:T(8,128)(2,1)S(1)} all-gather(bf16[4,64,64]{2,1,0:T(8,128)(2,1)} %param.12), channel_id=1, replica_groups=mesh['dp'=16,'fsdp'=16] {'dp'}, dimensions={0}, use_global_device_ids=true | all-gather | bytes 557056 | tf_op jit(solution)/shard_map/all_gather | solution.py:45
  79.4 0.6 gather_fusion
  80.1 0.6 broadcast_select_fusion.1
  80.8 0.8 constant_dynamic-slice_fusion.1
  81.7 0.2 reduce-window.4
  82.0 58.8 %all-gather.11.cloned.1.call-done = bf16[8192,512]{0,1:T(8,128)(2,1)} async-done(((bf16[512,512]{0,1:T(8,128)(2,1)}), bf16[8192,512]{0,1:T(8,128)(2,1)}) %all-gather.11.cloned.1.call-update) | async-done | bytes 8388624 | tf_op jit(solution)/shard_map/all_gather | solution.py:54
  140.8 8.8 %multiply_convert_fusion = bf16[512,1024]{0,1:T(8,128)(2,1)} fusion(bf16[256,1024]{1,0:T(8,128)(2,1)S(1)} %copy-done, pred[256,512]{0,1:T(32,128)(4,1)S(1)} %bitcast.57, bf16[8192,512]{0,1:T(8,128)(2,1)} %all-gather.11.cloned.1.call-done, bf16[256,8192]{1,0:T(8,128)(2,1)} %param.8), kind=kOutput, calls=%fused_computation.7 | convolution fusion | flops 2417229824 | bytes 14286848 | tf_op jit(solution)/shard_map/dot_general | solution.py:84
  149.6 40.8 %all-gather.7.cloned.1.call-done = bf16[512,1024]{0,1:T(8,128)(2,1)} async-done(((bf16[512,64]{0,1:T(8,128)(2,1)}), bf16[512,1024]{0,1:T(8,128)(2,1)}) %all-gather.7.cloned.1.call-update) | async-done | bytes 1048592 | tf_op jit(solution)/shard_map/all_gather | solution.py:55
  190.4 1.7 fusion.5
  192.1 7.8 %fusion = bf16[8192,512]{0,1:T(8,128)(2,1)} fusion(bf16[256,512]{0,1:T(8,128)(2,1)S(1)} %fusion.5, bf16[256,8192]{1,0:T(8,128)(2,1)} %param.8), kind=kOutput, calls=%fused_computation.3 | convolution fusion | flops 2151677952 | bytes 12845056 | tf_op jit(solution)/shard_map/dot_general | solution.py:81
  199.9 71.4 %reduce-scatter.9.cloned.1.call-done = bf16[512,64]{0,1:T(8,128)(2,1)} async-done(((bf16[512,1024]{0,1:T(8,128)(2,1)}), bf16[512,64]{0,1:T(8,128)(2,1)}) %reduce-scatter.9.cloned.1.call-update) | async-done | bytes 65552 | tf_op jit(solution)/shard_map/reduce_scatter | solution.py:91
  271.4 1.0 reshape.78
  272.5 0.5 convolution_convert_fusion.2
  273.1 1.7 copy.30
  274.8 90.5 %reduce-scatter.5.cloned.1.call-done = bf16[512,512]{0,1:T(8,128)(2,1)} async-done(((bf16[8192,512]{0,1:T(8,128)(2,1)}), bf16[512,512]{0,1:T(8,128)(2,1)}) %reduce-scatter.5.cloned.1.call-update) | async-done | bytes 524304 | tf_op jit(solution)/shard_map/reduce_scatter | solution.py:88
  365.3 2.4 convolution_convert_fusion.1
  367.7 4.4 copy.28
  372.2 0.2 all-gather.5.cloned.1.call-start
  372.4 0.5 all-gather.5.cloned.1.call-update
  372.9 9.0 %fusion.20 = f32[256,8192]{1,0:T(8,128)} fusion(bf16[256,512]{0,1:T(8,128)(2,1)S(1)} %fusion.5, bf16[8192,512]{0,1:T(8,128)(2,1)} %all-gather.11.cloned.1.call-done), kind=kOutput, calls=%fused_computation.42 | convolution fusion | flops 2147483648 | bytes 17039360 | tf_op jit(solution)/shard_map/dot_general | solution.py:77
  381.9 41.0 %reduce-scatter.11.cloned.1.call-done = bf16[4,64,64]{2,1,0:T(8,128)(2,1)} async-done(((bf16[64,64,64]{2,1,0:T(8,128)(2,1)}), bf16[4,64,64]{2,1,0:T(8,128)(2,1)}) %reduce-scatter.11.cloned.1.call-update) | async-done | bytes 32784 | tf_op jit(solution)/shard_map/reduce_scatter | solution.py:113
  422.9 1.5 convert_multiply_fusion.1
  424.4 62.8 %reduce-scatter.7.cloned.1.call-done = bf16[4,512,64]{1,2,0:T(8,128)(2,1)} async-done(((bf16[64,512,64]{1,2,0:T(8,128)(2,1)}), bf16[4,512,64]{1,2,0:T(8,128)(2,1)}) %reduce-scatter.7.cloned.1.call-update) | async-done | bytes 262160 | tf_op jit(solution)/shard_map/reduce_scatter | solution.py:110
  487.2 1.8 convert_multiply_fusion
  489.0 118.6 %all-gather.5.cloned.1.call-done = bf16[8192,1024]{1,0:T(8,128)(2,1)} async-done(((bf16[512,1024]{1,0:T(8,128)(2,1)}), bf16[8192,1024]{1,0:T(8,128)(2,1)}) %all-gather.5.cloned.1.call-update) | async-done | bytes 16777232 | tf_op jit(solution)/shard_map/all_gather | solution.py:73
  607.6 12.3 %fusion.1 = bf16[256,8192]{1,0:T(8,128)(2,1)} fusion(f32[256,8192]{1,0:T(8,128)} %fusion.20, bf16[256,1024]{1,0:T(8,128)(2,1)S(1)} %copy-done, bf16[8192,1024]{1,0:T(8,128)(2,1)} %all-gather.5.cloned.1.call-done), kind=kOutput, calls=%fused_computation.5 | convolution fusion | flops 4299161600 | bytes 29884416 | tf_op jit(solution)/shard_map/dot_general | solution.py:71
  (27 shorter events, 1.1 us)
Async XLA Ops:
  7.2 133.6 %copy-start = (bf16[256,1024]{1,0:T(8,128)(2,1)S(1)}, bf16[256,1024]{1,0:T(8,128)(2,1)}, u32[]{:S(2)}) copy-start(bf16[256,1024]{1,0:T(8,128)(2,1)} %param.9) | copy-start | bytes 1572868
  7.2 49.0 %all-gather.9.cloned.1.call-start = ((), (), s32[]{:S(2)}) async-start(), calls=%async_computation.6 | async-start | bytes 4456448 | tf_op jit(solution)/shard_map/all_gather | solution.py:44
  7.9 132.8 %all-gather.11.cloned.1.call-start = ((), (), s32[]{:S(2)}) async-start(), calls=%async_computation.7 | async-start | bytes 8912896 | tf_op jit(solution)/shard_map/all_gather | solution.py:54
  59.9 130.5 %all-gather.7.cloned.1.call-start = ((), (), s32[]{:S(2)}) async-start(), calls=%async_computation.5 | async-start | bytes 1114112 | tf_op jit(solution)/shard_map/all_gather | solution.py:55
  80.8 190.6 %reduce-scatter.9.cloned.1.call-start = ((), (), s32[]{:S(2)}) async-start(), calls=%async_computation.10 | async-start | bytes 1114112 | tf_op jit(solution)/shard_map/reduce_scatter | solution.py:91
  149.6 215.8 %reduce-scatter.5.cloned.1.call-start = ((), (), s32[]{:S(2)}) async-start(), calls=%async_computation.8 | async-start | bytes 8912896 | tf_op jit(solution)/shard_map/reduce_scatter | solution.py:88
  199.9 223.0 %reduce-scatter.11.cloned.1.call-start = ((), (), s32[]{:S(2)}) async-start(), calls=%async_computation.11 | async-start | bytes 1114112 | tf_op jit(solution)/shard_map/reduce_scatter | solution.py:113
  274.8 212.4 %reduce-scatter.7.cloned.1.call-start = ((), (), s32[]{:S(2)}) async-start(), calls=%async_computation.9 | async-start | bytes 4456448 | tf_op jit(solution)/shard_map/reduce_scatter | solution.py:110
  372.2 235.5 %all-gather.5.cloned.1.call-start = ((), (), s32[]{:S(2)}) async-start(), calls=%async_computation.4 | async-start | bytes 17825792 | tf_op jit(solution)/shard_map/all_gather | solution.py:73
Sparse Core Ops, SparseCore 0:
  9.8 46.3 all-gather.8
  60.0 80.6 all-gather.10
  143.7 46.5 all-gather.6
  194.3 77.0 reduce-scatter.8
  275.4 89.8 reduce-scatter.4
  367.9 54.9 reduce-scatter.10
  426.0 61.1 reduce-scatter.6
  489.6 117.9 all-gather.4
where the time goes:
time: 627 us
  waiting for transfers between devices  532 us (85%)
  matrix products  42.5 us (7%)
  blocking collectives  19.3 us (3%)
  between operations  14.2 us (2%)
  local copies, waits for them, and re-layouts  12.5 us (2%)
    all_gather x1, waiting for transfers between devices, local(): lax.all_gather(value_weight, 'fsdp', axis=0, tiled=True)  119 us
    reduce_scatter x1, waiting for transfers between devices, local(): lax.psum_scatter(part_down.astype(jnp.bfloat16), 'fsdp', scatter_dimensio...  90.5 us
    reduce_scatter x1, waiting for transfers between devices, local(): lax.psum_scatter(partial_up_gradient.astype(jnp.bfloat16), 'fsdp', scatte...  71.4 us
    reduce_scatter x1, waiting for transfers between devices, local(): lax.psum_scatter(table_down.astype(jnp.bfloat16), 'dp', scatter_dimension...  62.8 us
    all_gather x1, waiting for transfers between devices, local(): lax.all_gather(down_cols, 'fsdp', axis=0, tiled=True)  58.8 us
    all_gather x1, waiting for transfers between devices, local(): lax.all_gather(adapter_down_weight, 'dp', axis=0, tiled=True)  46.4 us
    reduce_scatter x1, waiting for transfers between devices, local(): lax.psum_scatter(table_up.astype(jnp.bfloat16), 'dp', scatter_dimension=0...  41 us
    all_gather x1, waiting for transfers between devices, local(): lax.all_gather(up_rows, 'fsdp', axis=1, tiled=True)  40.8 us
  transfers between devices with their start and end apart: 8, of which 8 were waited for; matrix products, arithmetic and copies ran while one was open for 7% of the time, Pallas kernels for 0%

commit v1 on v0

--- a/solution.py
+++ b/solution.py
@@ -52,7 +52,9 @@
     up_rows = segment_up_weight.reshape(slot_count * rank_space_width, value_width_piece)
     down_full, up_full = (
         lax.all_gather(down_cols, "fsdp", axis=0, tiled=True),
-        lax.all_gather(up_rows, "fsdp", axis=1, tiled=True),
+        jnp.concatenate(
+            lax.all_to_all(jnp.stack([up_rows] * lax.axis_size("fsdp")), "fsdp", 0, 0), axis=1
+        ),
     )
     my_lengths = lax.dynamic_index_in_dim(segment_lengths, me_bin, 0, keepdims=False)
     positions = me_piece * rows_here + jnp.arange(rows_here, dtype=jnp.int32)

time: 627 us -> 585 us (0.933)
  waiting for transfers between devices: 532 us -> 484 us
  starting transfers between devices: 0.51 us -> 6.99 us
    all_gather x1 -> x0, waiting for transfers between devices: 40.8 us -> none  [local(): lax.all_gather(up_rows, 'fsdp', axis=1, tiled=True)]
    all_gather x1, waiting for transfers between devices: 58.8 us -> 36.8 us  [local(): lax.all_gather(down_cols, 'fsdp', axis=0, tiled=True)]
    all_to_all x0 -> x1, waiting for transfers between devices: none -> 16.3 us  [local(): lax.all_to_all(jnp.stack([up_rows] * lax.axis_size('fsdp')), 'fsdp', 0, 0)]
    reduce_scatter x1, waiting for transfers between devices: 41 us -> 56.9 us  [local(): lax.psum_scatter(table_up.astype(jnp.bfloat16), 'dp', scatter_dimension=0...]
    reduce_scatter x1, waiting for transfers between devices: 62.8 us -> 50.6 us  [local(): lax.psum_scatter(table_down.astype(jnp.bfloat16), 'dp', scatter_dimension...]
    reduce_scatter x1, waiting for transfers between devices: 90.5 us -> 83.9 us  [local(): lax.psum_scatter(part_down.astype(jnp.bfloat16), 'fsdp', scatter_dimensio...]
    all_to_all x0 -> x1, starting transfers between devices: none -> 6.53 us  [local(): lax.all_to_all(jnp.stack([up_rows] * lax.axis_size('fsdp')), 'fsdp', 0, 0)]
where the time goes in v1:
time: 585 us
  waiting for transfers between devices  484 us (83%)
  matrix products  41.4 us (7%)
  blocking collectives  19.3 us (3%)
  between operations  14.3 us (2%)
  local copies, waits for them, and re-layouts  12.9 us (2%)
  starting transfers between devices  6.99 us (1%)
    all_gather x1, waiting for transfers between devices, local(): lax.all_gather(value_weight, 'fsdp', axis=0, tiled=True)  119 us
    reduce_scatter x1, waiting for transfers between devices, local(): lax.psum_scatter(part_down.astype(jnp.bfloat16), 'fsdp', scatter_dimensio...  83.9 us
    reduce_scatter x1, waiting for transfers between devices, local(): lax.psum_scatter(partial_up_gradient.astype(jnp.bfloat16), 'fsdp', scatte...  73.3 us
    reduce_scatter x1, waiting for transfers between devices, local(): lax.psum_scatter(table_up.astype(jnp.bfloat16), 'dp', scatter_dimension=0...  56.9 us
    reduce_scatter x1, waiting for transfers between devices, local(): lax.psum_scatter(table_down.astype(jnp.bfloat16), 'dp', scatter_dimension...  50.6 us
    all_gather x1, waiting for transfers between devices, local(): lax.all_gather(adapter_down_weight, 'dp', axis=0, tiled=True)  46.4 us
    all_gather x1, waiting for transfers between devices, local(): lax.all_gather(down_cols, 'fsdp', axis=0, tiled=True)  36.8 us
    all_gather x1, blocking collectives, local(): lax.all_gather(adapter_up_weight, 'dp', axis=0, tiled=True)  19.3 us
  transfers between devices with their start and end apart: 8, of which 8 were waited for; matrix products, arithmetic and copies ran while one was open for 7% of the time, Pallas kernels for 0%

profile of v1, /device:TPU:1, one launch (start us, length us, event | category | flops | bytes accessed | tf_op | source)
XLA Modules:
  0.0 584.8 jit_solution(4447156965514724474)
XLA Ops:
  7.2 0.7 all-gather.6.cloned.1.call-update
  8.0 0.8 copy.32
  8.7 1.1 select_reduce_fusion
  9.9 46.4 %all-gather.6.cloned.1.call-done = bf16[64,512,64]{1,2,0:T(8,128)(2,1)} async-done(((bf16[4,512,64]{1,2,0:T(8,128)(2,1)}), bf16[64,512,64]{1,2,0:T(8,128)(2,1)}) %all-gather.6.cloned.1.call-update) | async-done | bytes 4194320 | tf_op jit(solution)/shard_map/all_gather | solution.py:44
  56.2 2.8 gather_fusion.1
  59.0 0.9 broadcast_select_fusion
  60.1 19.3 %all_gather.13 = bf16[64,64,64]{2,1,0:T(8,128)(2,1)S(1)} all-gather(bf16[4,64,64]{2,1,0:T(8,128)(2,1)} %param.12), channel_id=1, replica_groups=mesh['dp'=16,'fsdp'=16] {'dp'}, dimensions={0}, use_global_device_ids=true | all-gather | bytes 557056 | tf_op jit(solution)/shard_map/all_gather | solution.py:45
  79.4 0.6 gather_fusion
  80.1 1.1 stack.3
  81.2 6.5 %all-to-all-start = ((bf16[16,512,64]{1,2,0:T(8,128)(2,1)}), bf16[16,512,64]{1,2,0:T(8,128)(2,1)S(1)}, u32[]{:S(2)}, u32[]{:S(2)}) async-start(bf16[16,512,64]{1,2,0:T(8,128)(2,1)} %stack.3), calls=%async_computation | async-start | bytes 2097152 | tf_op jit(solution)/shard_map/all_to_all | solution.py:56
  87.9 0.2 reduce-window.4
  88.2 16.3 %all-to-all-done = bf16[16,512,64]{1,2,0:T(8,128)(2,1)S(1)} async-done(((bf16[16,512,64]{1,2,0:T(8,128)(2,1)}), bf16[16,512,64]{1,2,0:T(8,128)(2,1)S(1)}, u32[]{:S(2)}, u32[]{:S(2)}) %all-to-all-start) | async-done | bytes 1048608 | tf_op jit(solution)/shard_map/all_to_all | solution.py:56
  104.5 0.5 fusion.5
  105.0 7.8 %fusion = bf16[8192,512]{0,1:T(8,128)(2,1)} fusion(bf16[256,512]{0,1:T(8,128)(2,1)S(1)} %fusion.5, bf16[256,8192]{1,0:T(8,128)(2,1)} %param.8), kind=kOutput, calls=%fused_computation.3 | convolution fusion | flops 2151677952 | bytes 12845056 | tf_op jit(solution)/shard_map/dot_general | solution.py:83
  112.9 36.8 %all-gather.8.cloned.1.call-done = bf16[8192,512]{0,1:T(8,128)(2,1)} async-done(((bf16[512,512]{0,1:T(8,128)(2,1)}), bf16[8192,512]{0,1:T(8,128)(2,1)}) %all-gather.8.cloned.1.call-update) | async-done | bytes 8388624 | tf_op jit(solution)/shard_map/all_gather | solution.py:54
  149.7 8.9 %multiply_convert_fusion = bf16[512,1024]{0,1:T(8,128)(2,1)} fusion(bf16[256,1024]{1,0:T(8,128)(2,1)S(1)} %copy-done, pred[256,512]{0,1:T(32,128)(4,1)S(1)} %bitcast.62, bf16[8192,512]{0,1:T(8,128)(2,1)} %all-gather.8.cloned.1.call-done, bf16[256,8192]{1,0:T(8,128)(2,1)} %param.8), kind=kOutput, calls=%fused_computation.7 | convolution fusion | flops 2417229824 | bytes 14286848 | tf_op jit(solution)/shard_map/dot_general | solution.py:86
  158.6 83.9 %reduce-scatter.5.cloned.1.call-done = bf16[512,512]{0,1:T(8,128)(2,1)} async-done(((bf16[8192,512]{0,1:T(8,128)(2,1)}), bf16[512,512]{0,1:T(8,128)(2,1)}) %reduce-scatter.5.cloned.1.call-update) | async-done | bytes 524304 | tf_op jit(solution)/shard_map/reduce_scatter | solution.py:90
  242.6 2.4 convolution_convert_fusion.1
  245.0 4.4 copy.35
  249.4 0.2 reduce-scatter.11.cloned.1.call-start
  249.6 73.3 %reduce-scatter.9.cloned.1.call-done = bf16[512,64]{0,1:T(8,128)(2,1)} async-done(((bf16[512,1024]{0,1:T(8,128)(2,1)}), bf16[512,64]{0,1:T(8,128)(2,1)}) %reduce-scatter.9.cloned.1.call-update) | async-done | bytes 65552 | tf_op jit(solution)/shard_map/reduce_scatter | solution.py:93
  322.9 1.0 reshape.87
  324.0 0.5 convolution_convert_fusion.2
  324.6 1.7 copy.37
  326.3 0.7 all-gather.4.cloned.1.call-update
  327.1 9.0 %fusion.20 = f32[256,8192]{1,0:T(8,128)} fusion(bf16[256,512]{0,1:T(8,128)(2,1)S(1)} %fusion.5, bf16[8192,512]{0,1:T(8,128)(2,1)} %all-gather.8.cloned.1.call-done), kind=kOutput, calls=%fused_computation.42 | convolution fusion | flops 2147483648 | bytes 17039360 | tf_op jit(solution)/shard_map/dot_general | solution.py:79
  336.0 50.6 %reduce-scatter.7.cloned.1.call-done = bf16[4,512,64]{1,2,0:T(8,128)(2,1)} async-done(((bf16[64,512,64]{1,2,0:T(8,128)(2,1)}), bf16[4,512,64]{1,2,0:T(8,128)(2,1)}) %reduce-scatter.7.cloned.1.call-update) | async-done | bytes 262160 | tf_op jit(solution)/shard_map/reduce_scatter | solution.py:112
  386.6 1.8 convert_multiply_fusion
  388.4 56.9 %reduce-scatter.11.cloned.1.call-done = bf16[4,64,64]{2,1,0:T(8,128)(2,1)} async-done(((bf16[64,64,64]{2,1,0:T(8,128)(2,1)}), bf16[4,64,64]{2,1,0:T(8,128)(2,1)}) %reduce-scatter.11.cloned.1.call-update) | async-done | bytes 32784 | tf_op jit(solution)/shard_map/reduce_scatter | solution.py:115
  445.3 1.5 convert_multiply_fusion.1
  446.8 118.8 %all-gather.4.cloned.1.call-done = bf16[8192,1024]{1,0:T(8,128)(2,1)} async-done(((bf16[512,1024]{1,0:T(8,128)(2,1)}), bf16[8192,1024]{1,0:T(8,128)(2,1)}) %all-gather.4.cloned.1.call-update) | async-done | bytes 16777232 | tf_op jit(solution)/shard_map/all_gather | solution.py:75
  565.6 12.3 %fusion.1 = bf16[256,8192]{1,0:T(8,128)(2,1)} fusion(f32[256,8192]{1,0:T(8,128)} %fusion.20, bf16[256,1024]{1,0:T(8,128)(2,1)S(1)} %copy-done, bf16[8192,1024]{1,0:T(8,128)(2,1)} %all-gather.4.cloned.1.call-done), kind=kOutput, calls=%fused_computation.5 | convolution fusion | flops 4299161600 | bytes 29884416 | tf_op jit(solution)/shard_map/dot_general | solution.py:73
  (29 shorter events, 1.1 us)
Async XLA Ops:
  7.2 97.3 %copy-start = (bf16[256,1024]{1,0:T(8,128)(2,1)S(1)}, bf16[256,1024]{1,0:T(8,128)(2,1)}, u32[]{:S(2)}) copy-start(bf16[256,1024]{1,0:T(8,128)(2,1)} %param.9) | copy-start | bytes 1572868
  7.2 80.6 %copy-start.1 = (s32[16,8]{0,1:T(8,128)S(1)}, s32[16,8]{0,1:T(8,128)}, u32[]{:S(2)}) copy-start(s32[16,8]{0,1:T(8,128)} %param.14) | copy-start | bytes 1540
  7.2 49.0 %all-gather.6.cloned.1.call-start = ((), (), s32[]{:S(2)}) async-start(), calls=%async_computation.6 | async-start | bytes 4456448 | tf_op jit(solution)/shard_map/all_gather | solution.py:44
  7.9 141.8 %all-gather.8.cloned.1.call-start = ((), (), s32[]{:S(2)}) async-start(), calls=%async_computation.7 | async-start | bytes 8912896 | tf_op jit(solution)/shard_map/all_gather | solution.py:54
  81.2 23.3 %all-to-all-start = ((bf16[16,512,64]{1,2,0:T(8,128)(2,1)}), bf16[16,512,64]{1,2,0:T(8,128)(2,1)S(1)}, u32[]{:S(2)}, u32[]{:S(2)}) async-start(bf16[16,512,64]{1,2,0:T(8,128)(2,1)} %stack.3), calls=%async_computation | async-start | bytes 2097152 | tf_op jit(solution)/shard_map/all_to_all | solution.py:56
  87.7 154.9 %reduce-scatter.5.cloned.1.call-start = ((), (), s32[]{:S(2)}) async-start(), calls=%async_computation.8 | async-start | bytes 8912896 | tf_op jit(solution)/shard_map/reduce_scatter | solution.py:90
  112.8 210.1 %reduce-scatter.9.cloned.1.call-start = ((), (), s32[]{:S(2)}) async-start(), calls=%async_computation.10 | async-start | bytes 1114112 | tf_op jit(solution)/shard_map/reduce_scatter | solution.py:93
  158.6 228.0 %reduce-scatter.7.cloned.1.call-start = ((), (), s32[]{:S(2)}) async-start(), calls=%async_computation.9 | async-start | bytes 4456448 | tf_op jit(solution)/shard_map/reduce_scatter | solution.py:112
  249.4 195.8 %reduce-scatter.11.cloned.1.call-start = ((), (), s32[]{:S(2)}) async-start(), calls=%async_computation.11 | async-start | bytes 1114112 | tf_op jit(solution)/shard_map/reduce_scatter | solution.py:115
  326.3 239.3 %all-gather.4.cloned.1.call-start = ((), (), s32[]{:S(2)}) async-start(), calls=%async_computation.5 | async-start | bytes 17825792 | tf_op jit(solution)/shard_map/all_gather | solution.py:75
Sparse Core Ops, SparseCore 0:
  9.9 46.3 all-gather.5
  60.0 89.5 all-gather.7
  153.4 89.1 reduce-scatter.4
  245.9 76.9 reduce-scatter.8
  326.0 60.5 reduce-scatter.6
  389.1 56.0 reduce-scatter.10
  447.7 117.8 all-gather.3
